TPU v7x, 32 devices: a whole 2x2x4 slice. The times are simulated.
32 devices in a mesh: tm: 16 (over z, y, core), mom: 2 (over x).
Axes of the slice: x: 2, y: 2, z: 4, core: 2. Of those that a mesh axis runs over, the one named last changes fastest.
Arguments:
- sink_solutions: bfloat16 [16, 2, 512, 512], P('tm'), may hold values from -0.44921875 to 0.44921875
- noise_sources: bfloat16 [16, 2, 512, 512], P('tm'), may hold values from -0.44921875 to 0.44921875
- elementals: bfloat16 [2, 16, 2, 128, 128], P('mom', 'tm'), may hold values from -0.375 to 0.375
- pairs: int32 [2, 2], P('mom'), may hold values from 0 to 1
Outputs:
- blocks: bfloat16 [16, 4, 2, 2, 512, 512], P('tm', None, 'mom')
Inputs may be any that keep to these rules, and one draw needn't show every extreme that they name: `pairs`: entries are operator indices.
All inputs are finite; a program needn't handle non-finite values.
Results may differ from a plain program's by a relative error of at most 0.007.
Values may be sent and summed in bfloat16 or wider, within the bound.
A program may use at most 64 MiB of HBM per device.

v0:
```python
import jax
import jax.numpy as jnp
from jax import lax
from jax.sharding import PartitionSpec as P

NSEP = 4


def shifted(block, axis, distance):
    devices = range(lax.axis_size(axis))
    route = [((i - distance) % len(devices), i) for i in devices]
    return lax.ppermute(block, axis, route)


def transpose_product(left_mat, right_mat):
    return lax.dot_general(
        left_mat, right_mat, (((1,), (1,)), ((), ())), preferred_element_type=jnp.float32
    )


def complex_product(left_mat, right_mat):
    real_part = jnp.dot(left_mat[0], right_mat[0], preferred_element_type=jnp.float32) - jnp.dot(
        left_mat[1], right_mat[1], preferred_element_type=jnp.float32
    )
    imag_part = jnp.dot(left_mat[0], right_mat[1], preferred_element_type=jnp.float32) + jnp.dot(
        left_mat[1], right_mat[0], preferred_element_type=jnp.float32
    )
    return jnp.stack([real_part, imag_part])


def meson_function(sink_piece, noise_part, elemental):
    dilution_rows = sink_piece.shape[1]
    total_width = sink_piece.shape[2]
    eigenvector_count = elemental.shape[1]
    spinor_rows = sink_piece.reshape(
        2, dilution_rows * (total_width // eigenvector_count), eigenvector_count
    )
    applied_real = transpose_product(spinor_rows[0], elemental[0]) - transpose_product(
        spinor_rows[1], elemental[1]
    )
    applied_imaginary = transpose_product(spinor_rows[0], elemental[1]) + transpose_product(
        spinor_rows[1], elemental[0]
    )
    applied_result = (
        jnp.stack([applied_real, applied_imaginary])
        .reshape(2, dilution_rows, total_width)
        .astype(jnp.bfloat16)
    )
    meson_re = transpose_product(noise_part[0], applied_result[0]) + transpose_product(
        noise_part[1], applied_result[1]
    )
    meson_im = transpose_product(noise_part[0], applied_result[1]) - transpose_product(
        noise_part[1], applied_result[0]
    )
    return jnp.stack([meson_re, meson_im]).astype(jnp.bfloat16)


def local(sink_solutions, noise_sources, elementals, pairs):
    sink_piece = sink_solutions[0]
    noise_part = noise_sources[0]
    operator_sink = pairs[0, 0]
    operator_source = pairs[0, 1]
    held_elementals = elementals[:, 0]
    zeros_elemental = jnp.zeros_like(held_elementals[0])
    carried = (zeros_elemental, zeros_elemental)
    fragment = lax.all_gather(held_elementals, "mom", axis=0, tiled=True)
    row_count = fragment.shape[0]
    selected = []
    for position, wanted in enumerate((operator_sink, operator_source)):
        inside = (wanted >= 0) & (wanted < row_count)
        candidate = lax.dynamic_index_in_dim(
            fragment, jnp.clip(wanted, 0, row_count - 1), 0, keepdims=False
        )
        selected.append(jnp.where(inside, candidate, carried[position]))
    sink_elemental, source_elemental = tuple(selected)
    later_meson = meson_function(sink_piece, noise_part, sink_elemental)
    source_meson = meson_function(sink_piece, noise_part, source_elemental)
    arrived = []
    current_meson = later_meson
    for separation in range(NSEP):
        current_meson = shifted(current_meson, "tm", -1)
        arrived.append(current_meson)
    results = jnp.stack(
        [complex_product(moved_meson, source_meson).astype(jnp.bfloat16) for moved_meson in arrived]
    )
    return results[None, :, None]


def solution(mesh):
    return jax.shard_map(
        local,
        mesh=mesh,
        in_specs=(
            P("tm", None, None, None),
            P("tm", None, None, None),
            P("mom", "tm", None, None, None),
            P("mom", None),
        ),
        out_specs=P("tm", None, "mom", None, None, None),
        check_vma=False,
    )
```

profile of v0, /device:TPU:0, one launch (start us, length us, event | category | flops | bytes accessed | tf_op | source)
XLA Modules:
  0.0 95.7 jit_solution(5581900416180342018)
XLA Ops:
  0.0 1.3 %fusion.63 = (s32[1,1]{1,0:T(1,128)}, s32[1,1]{1,0:T(1,128)}) fusion(s32[1,2]{1,0:T(1,128)} %param.7), kind=kLoop, calls=%fused_computation.95 | loop fusion | bytes 16 | tf_op jit(solution)/shard_map/slice | solution.py:61
  4.9 6.1 %all-gather = bf16[2,1,2,128,128]{4,3,2,1,0:T(8,128)(2,1)S(1)} all-gather(bf16[1,1,2,128,128]{4,3,2,1,0:T(8,128)(2,1)} %param.6), channel_id=2, replica_groups=mesh['tm'=16,'mom'=2] {'mom'}, dimensions={0}, use_global_device_ids=true | all-gather | bytes 196608 | tf_op jit(solution)/shard_map/all_gather | solution.py:66
  11.1 1.3 %fusion.62 = (bf16[1,1,512,512]{3,2,1,0:T(8,128)(2,1)S(1)}, bf16[1,1,512,512]{3,2,1,0:T(8,128)(2,1)S(1)}) fusion(bf16[1,2,512,512]{3,2,1,0:T(8,128)(2,1)} %param.4), kind=kLoop, calls=%fused_computation.94 | loop fusion | bytes 2097152 | tf_op jit(solution)/shard_map/slice | solution.py:39
  13.0 1.3 %fusion.58 = f32[128,2048]{1,0:T(8,128)} fusion(bf16[2048,128]{1,0:T(8,128)(2,1)S(1)} %squeeze.47, bf16[1,2,128,128]{3,2,1,0:T(8,128)(2,1)S(1)} %get-tuple-element.7), kind=kOutput, calls=%fused_computation.90 | convolution fusion | flops 67108864 | bytes 1605632 | tf_op jit(solution)/shard_map/dot_general | solution.py:16
  14.6 1.1 %fusion.6 = bf16[2048,128]{0,1:T(8,128)(2,1)} fusion(f32[128,2048]{1,0:T(8,128)S(1)} %fusion.59, bf16[2048,128]{1,0:T(8,128)(2,1)S(1)} %squeeze.49, bf16[1,2,128,128]{3,2,1,0:T(8,128)(2,1)S(1)} %get-tuple-element.7), kind=kOutput, calls=%fused_computation.11 | convolution fusion | flops 67633152 | bytes 2129920 | tf_op jit(solution)/shard_map/dot_general | solution.py:16
  15.7 1.3 %copy.12 = bf16[2048,128]{1,0:T(8,128)(2,1)S(1)} copy(bf16[2048,128]{0,1:T(8,128)(2,1)} %fusion.6) | data formatting | bytes 1048576 | tf_op jit(solution)/shard_map/add | solution.py:41
  17.3 1.5 %fusion.7 = bf16[2048,128]{0,1:T(8,128)(2,1)S(1)} fusion(f32[128,2048]{1,0:T(8,128)} %fusion.58, bf16[2048,128]{1,0:T(8,128)(2,1)S(1)} %squeeze.49, bf16[1,2,128,128]{3,2,1,0:T(8,128)(2,1)S(1)} %get-tuple-element.7), kind=kOutput, calls=%fused_computation.12 | convolution fusion | flops 67633152 | bytes 2129920 | tf_op jit(solution)/shard_map/dot_general | solution.py:16
  18.9 1.0 %copy.11 = bf16[2048,128]{1,0:T(8,128)(2,1)} copy(bf16[2048,128]{0,1:T(8,128)(2,1)S(1)} %fusion.7) | data formatting | bytes 1048576 | tf_op jit(solution)/shard_map/sub | solution.py:38
  19.9 1.4 %squeeze.50 = bf16[512,512]{1,0:T(8,128)(2,1)S(1)} reshape(bf16[2048,128]{1,0:T(8,128)(2,1)} %copy.11) | data formatting | bytes 1048576 | tf_op jit(solution)/shard_map/squeeze | solution.py:49
  23.1 1.1 %pad_maximum_fusion = bf16[2,512,512]{1,2,0:T(8,128)(2,1)} fusion(bf16[1,512,512]{1,2,0:T(8,128)(2,1)S(1)} %fusion.28, bf16[1,512,512]{1,2,0:T(8,128)(2,1)S(1)} %fusion.29), kind=kLoop, calls=%fused_computation.47 | loop fusion | flops 524288 | bytes 2097152 | tf_op jit(solution)/shard_map/stack | solution.py:55
  24.2 3.3 %collective-permute-start = (bf16[2,512,512]{1,2,0:T(8,128)(2,1)}, bf16[2,512,512]{1,2,0:T(8,128)(2,1)}, u32[]{:S(2)}, u32[]{:S(2)}) collective-permute-start(bf16[2,512,512]{1,2,0:T(8,128)(2,1)} %pad_maximum_fusion), channel_id=1, source_target_pairs={{2,0},{4,2},{6,4},{8,6},{10,8},{12,10},{14,12},{16,14},{18,16},{20... | collective-permute-start | bytes 3145736 | tf_op jit(solution)/shard_map/ppermute | solution.py:12
  30.9 9.3 %collective-permute-done = bf16[2,512,512]{1,2,0:T(8,128)(2,1)} collective-permute-done((bf16[2,512,512]{1,2,0:T(8,128)(2,1)}, bf16[2,512,512]{1,2,0:T(8,128)(2,1)}, u32[]{:S(2)}, u32[]{:S(2)}) %collective-permute-start) | collective-permute-done | bytes 1048608 | tf_op jit(solution)/shard_map/ppermute | solution.py:12
  40.2 4.6 %collective-permute-start.1 = (bf16[2,512,512]{1,2,0:T(8,128)(2,1)}, bf16[2,512,512]{1,2,0:T(8,128)(2,1)S(1)}, u32[]{:S(2)}, u32[]{:S(2)}) collective-permute-start(bf16[2,512,512]{1,2,0:T(8,128)(2,1)} %collective-permute-done), channel_id=1, source_target_pairs={{2,0},{4,2},{6,4},{8,6},{10,8},{12,10},{14,12},{16,14},{18,16},{20... | collective-permute-start | bytes 3145736 | tf_op jit(solution)/shard_map/ppermute | solution.py:12
  45.7 1.5 %fusion.42 = f32[512,512]{1,0:T(8,128)S(1)} fusion(bf16[512,512]{1,0:T(8,128)(2,1)S(1)} %fusion.10, bf16[2,512,512]{1,2,0:T(8,128)(2,1)} %collective-permute-done), kind=kOutput, calls=%fused_computation.68 | convolution fusion | flops 268435456 | bytes 2097152 | tf_op jit(solution)/shard_map/dot_general | solution.py:25
  47.2 1.5 %fusion.43 = f32[512,512]{1,0:T(8,128)S(1)} fusion(bf16[512,512]{1,0:T(8,128)(2,1)S(1)} %fusion.12, bf16[2,512,512]{1,2,0:T(8,128)(2,1)} %collective-permute-done), kind=kOutput, calls=%fused_computation.69 | convolution fusion | flops 268435456 | bytes 2097152 | tf_op jit(solution)/shard_map/dot_general | solution.py:22
  48.8 8.6 %collective-permute-done.1 = bf16[2,512,512]{1,2,0:T(8,128)(2,1)S(1)} collective-permute-done((bf16[2,512,512]{1,2,0:T(8,128)(2,1)}, bf16[2,512,512]{1,2,0:T(8,128)(2,1)S(1)}, u32[]{:S(2)}, u32[]{:S(2)}) %collective-permute-start.1) | collective-permute-done | bytes 1048608 | tf_op jit(solution)/shard_map/ppermute | solution.py:12
  57.4 4.5 %collective-permute-start.2 = (bf16[2,512,512]{1,2,0:T(8,128)(2,1)S(1)}, bf16[2,512,512]{1,2,0:T(8,128)(2,1)S(1)}, u32[]{:S(2)}, u32[]{:S(2)}) collective-permute-start(bf16[2,512,512]{1,2,0:T(8,128)(2,1)S(1)} %collective-permute-done.1), channel_id=1, source_target_pairs={{2,0},{4,2},{6,4},{8,6},{10,8},{12,10},{14,12},{16,14},{18,16},{20... | collective-permute-start | bytes 3145736 | tf_op jit(solution)/shard_map/ppermute | solution.py:12
  61.9 1.5 %fusion.26 = bf16[1,1,512,512]{3,2,1,0:T(8,128)(2,1)S(1)} fusion(f32[512,512]{1,0:T(8,128)S(1)} %fusion.42, bf16[512,512]{1,0:T(8,128)(2,1)S(1)} %fusion.12, bf16[2,512,512]{1,2,0:T(8,128)(2,1)} %collective-permute-done), kind=kOutput, calls=%fused_computation.43 | convolution fusion | flops 268959744 | bytes 2621440 | tf_op jit(solution)/shard_map/dot_general | solution.py:25
  63.4 1.5 %fusion.27 = bf16[1,1,512,512]{3,2,1,0:T(8,128)(2,1)S(1)} fusion(f32[512,512]{1,0:T(8,128)S(1)} %fusion.43, bf16[512,512]{1,0:T(8,128)(2,1)S(1)} %fusion.10, bf16[2,512,512]{1,2,0:T(8,128)(2,1)} %collective-permute-done), kind=kOutput, calls=%fused_computation.44 | convolution fusion | flops 268959744 | bytes 2621440 | tf_op jit(solution)/shard_map/dot_general | solution.py:22
  65.0 0.5 fusion.44
  65.5 0.5 fusion.24
  65.9 0.5 fusion.45
  66.4 7.8 %collective-permute-done.2 = bf16[2,512,512]{1,2,0:T(8,128)(2,1)S(1)} collective-permute-done((bf16[2,512,512]{1,2,0:T(8,128)(2,1)S(1)}, bf16[2,512,512]{1,2,0:T(8,128)(2,1)S(1)}, u32[]{:S(2)}, u32[]{:S(2)}) %collective-permute-start.2) | collective-permute-done | bytes 1048608 | tf_op jit(solution)/shard_map/ppermute | solution.py:12
  74.2 4.6 %collective-permute-start.3 = (bf16[2,512,512]{1,2,0:T(8,128)(2,1)S(1)}, bf16[2,512,512]{1,2,0:T(8,128)(2,1)S(1)}, u32[]{:S(2)}, u32[]{:S(2)}) collective-permute-start(bf16[2,512,512]{1,2,0:T(8,128)(2,1)S(1)} %collective-permute-done.2), channel_id=1, source_target_pairs={{2,0},{4,2},{6,4},{8,6},{10,8},{12,10},{14,12},{16,14},{18,16},{20... | collective-permute-start | bytes 3145736 | tf_op jit(solution)/shard_map/ppermute | solution.py:12
  78.8 0.5 fusion.25
  79.8 0.5 fusion.22
  80.8 0.5 fusion.23
  81.3 9.9 %collective-permute-done.3 = bf16[2,512,512]{1,2,0:T(8,128)(2,1)S(1)} collective-permute-done((bf16[2,512,512]{1,2,0:T(8,128)(2,1)S(1)}, bf16[2,512,512]{1,2,0:T(8,128)(2,1)S(1)}, u32[]{:S(2)}, u32[]{:S(2)}) %collective-permute-start.3) | collective-permute-done | bytes 1048608 | tf_op jit(solution)/shard_map/ppermute | solution.py:12
  91.6 0.5 fusion.49
  92.1 0.5 fusion.20
  92.6 0.5 fusion.21
  93.1 2.6 %maximum_bitcast_fusion = bf16[1,4,1,2,512,512]{5,4,3,2,1,0:T(8,128)(2,1)} fusion(bf16[1,1,512,512]{3,2,1,0:T(8,128)(2,1)S(1)} %fusion.20, bf16[1,1,512,512]{3,2,1,0:T(8,128)(2,1)S(1)} %fusion.21, bf16[1,1,512,512]{3,2,1,0:T(8,128)(2,1)S(1)} %fusion.22, bf16[1,1,512,512]{3,2,1,0:T(8,128)(2,1)S(1)} %fusion.23, bf16[1,1,512,512]{3,2,1,0:T(8,128)(2,1)S(1)} %fusion.24, ...), kind=kLoop, calls=%fused_computation | loop fusion | flops 14680064 | bytes 8388608 | tf_op jit(solution)/shard_map/broadcast_in_dim | solution.py:86
  (26 shorter events, 8.8 us)
Async XLA Ops:
  14.6 6.6 %copy-start = (bf16[1,2,512,512]{3,2,1,0:T(8,128)(2,1)S(1)}, bf16[1,2,512,512]{3,2,1,0:T(8,128)(2,1)}, u32[]{:S(2)}) copy-start(bf16[1,2,512,512]{3,2,1,0:T(8,128)(2,1)} %param.5) | copy-start | bytes 3145732
  24.2 16.0 %collective-permute-start = (bf16[2,512,512]{1,2,0:T(8,128)(2,1)}, bf16[2,512,512]{1,2,0:T(8,128)(2,1)}, u32[]{:S(2)}, u32[]{:S(2)}) collective-permute-start(bf16[2,512,512]{1,2,0:T(8,128)(2,1)} %pad_maximum_fusion), channel_id=1, source_target_pairs={{2,0},{4,2},{6,4},{8,6},{10,8},{12,10},{14,12},{16,14},{18,16},{20... | collective-permute-start | bytes 3145736 | tf_op jit(solution)/shard_map/ppermute | solution.py:12
  40.2 17.2 %collective-permute-start.1 = (bf16[2,512,512]{1,2,0:T(8,128)(2,1)}, bf16[2,512,512]{1,2,0:T(8,128)(2,1)S(1)}, u32[]{:S(2)}, u32[]{:S(2)}) collective-permute-start(bf16[2,512,512]{1,2,0:T(8,128)(2,1)} %collective-permute-done), channel_id=1, source_target_pairs={{2,0},{4,2},{6,4},{8,6},{10,8},{12,10},{14,12},{16,14},{18,16},{20... | collective-permute-start | bytes 3145736 | tf_op jit(solution)/shard_map/ppermute | solution.py:12
  57.4 16.8 %collective-permute-start.2 = (bf16[2,512,512]{1,2,0:T(8,128)(2,1)S(1)}, bf16[2,512,512]{1,2,0:T(8,128)(2,1)S(1)}, u32[]{:S(2)}, u32[]{:S(2)}) collective-permute-start(bf16[2,512,512]{1,2,0:T(8,128)(2,1)S(1)} %collective-permute-done.1), channel_id=1, source_target_pairs={{2,0},{4,2},{6,4},{8,6},{10,8},{12,10},{14,12},{16,14},{18,16},{20... | collective-permute-start | bytes 3145736 | tf_op jit(solution)/shard_map/ppermute | solution.py:12
  74.2 16.9 %collective-permute-start.3 = (bf16[2,512,512]{1,2,0:T(8,128)(2,1)S(1)}, bf16[2,512,512]{1,2,0:T(8,128)(2,1)S(1)}, u32[]{:S(2)}, u32[]{:S(2)}) collective-permute-start(bf16[2,512,512]{1,2,0:T(8,128)(2,1)S(1)} %collective-permute-done.2), channel_id=1, source_target_pairs={{2,0},{4,2},{6,4},{8,6},{10,8},{12,10},{14,12},{16,14},{18,16},{20... | collective-permute-start | bytes 3145736 | tf_op jit(solution)/shard_map/ppermute | solution.py:12
where the time goes:
time: 96.2 us; the launch traced here: 95.7 us
  waiting for transfers between devices  35.5 us (37%)
  matrix products  21.1 us (22%)
  starting transfers between devices  17 us (18%)
  local copies, waits for them, and re-layouts  8.37 us (9%)
  blocking collectives  6.11 us (6%)
  between operations  3.9 us (4%)
  other arithmetic  3.69 us (4%)
    ppermute x4, waiting for transfers between devices, shifted(): return lax.ppermute(block, axis, route)  35.5 us
    ppermute x4, starting transfers between devices, shifted(): return lax.ppermute(block, axis, route)  17 us
    dot_general x16, matrix products, transpose_product(): lax.dot_general(left_mat, right_mat, (((1,), (1,)), ((), ())), preferred_...  9.13 us
    all_gather x1, blocking collectives, local(): fragment = lax.all_gather(held_elementals, 'mom', axis=0, tiled=True)  6.11 us
    dot_general x4, matrix products, complex_product(): jnp.dot(left_mat[0], right_mat[1], preferred_element_type=jnp.float32)  2.99 us
    dot_general x4, matrix products, complex_product(): jnp.dot(left_mat[0], right_mat[0], preferred_element_type=jnp.float32)  2.98 us
    dot_general x4, matrix products, complex_product(): jnp.dot(left_mat[1], right_mat[1], preferred_element_type=jnp.float32)  2.98 us
    dot_general x4, matrix products, complex_product(): jnp.dot(left_mat[1], right_mat[0], preferred_element_type=jnp.float32)  2.98 us
  transfers between devices with their start and end apart: 4, of which 4 were waited for; matrix products, arithmetic and copies ran while one was open for 15% of the time, Pallas kernels for 0%

commit v1 on v0

v1 whole, which is shorter than its diff:
```python
import functools

import jax
import jax.numpy as jnp
from jax import lax
from jax.experimental import pallas as pl
from jax.experimental.pallas import tpu as pltpu
from jax.sharding import PartitionSpec as P

NSEP = 4
MESH = pl.DeviceIdType.MESH
CHUNKS = 8


def dot(left, right):
    return jnp.dot(left, right, preferred_element_type=jnp.float32)


def kernel(
    n_times, n_mom, chunks,
    sink_hbm, noise_hbm, elem_hbm, pairs_ref, out_hbm,
    sink, noise, elems, weights, own, source, recv, staged,
    load_sem, elem_send, elem_recv, send_sem, recv_sem, out_sem,
):
    time = lax.axis_index("tm")
    mom = lax.axis_index("mom")
    odd = lax.rem(time, 2)
    upper = lax.rem(time // 2, 2)
    sibling = time + 1 - 2 * odd
    across = time + 2 - 4 * upper
    before = lax.rem(time + n_times - 4, n_times)
    after = lax.rem(time + 4, n_times)

    width = sink.shape[2]
    dil = sink.shape[1]
    ops = elem_hbm.shape[0]
    nev = elem_hbm.shape[3]
    spins = width // nev
    rows = dil // chunks

    own_elem = pltpu.make_async_copy(
        elem_hbm.at[:, 0], elems.at[pl.ds(mom * ops, ops)], load_sem.at[0]
    )
    own_elem.start()
    sink_load = pltpu.make_async_copy(sink_hbm.at[0], sink, load_sem.at[1])
    sink_load.start()
    noise_loads = [
        pltpu.make_async_copy(
            noise_hbm.at[0, part], noise.at[:, pl.ds(part * width, width)], load_sem.at[2 + part]
        )
        for part in range(2)
    ]
    for load in noise_loads:
        load.start()

    barrier = pltpu.get_barrier_semaphore()
    mom_peers = [lax.rem(mom + step, n_mom) for step in range(1, n_mom)]
    for peer in mom_peers:
        pl.semaphore_signal(barrier, inc=1, device_id=(time, peer), device_id_type=MESH)
    for peer in (sibling, across, before, after):
        pl.semaphore_signal(barrier, inc=1, device_id=(peer, mom), device_id_type=MESH)
    pl.semaphore_wait(barrier, n_mom - 1 + 4)

    elem_sends = []
    for step, peer in enumerate(mom_peers):
        send = pltpu.make_async_remote_copy(
            src_ref=elem_hbm.at[:, 0],
            dst_ref=elems.at[pl.ds(mom * ops, ops)],
            send_sem=elem_send.at[step],
            recv_sem=elem_recv.at[step],
            device_id=(time, peer),
            device_id_type=MESH,
        )
        send.start()
        elem_sends.append(send)
    own_elem.wait()
    sink_load.wait()
    for send in elem_sends:
        send.wait_recv()
    for load in noise_loads:
        load.wait()

    def fill_weights(which):
        chosen = elems[pairs_ref[0, which]]
        real, imag = chosen[0], chosen[1]
        left = jnp.concatenate(
            [jnp.concatenate([real, -imag], axis=1), jnp.concatenate([imag, real], axis=1)], axis=0
        )
        for spin in range(spins):
            cols = pl.ds(spin * nev, nev)
            right = jnp.concatenate([sink[0, :, cols], sink[1, :, cols]], axis=1)
            applied = lax.dot_general(
                left, right, (((1,), (1,)), ((), ())), preferred_element_type=jnp.float32
            ).astype(jnp.bfloat16)
            ap_re, ap_im = applied[:nev], applied[nev:]
            upper_rows = pl.ds(spin * nev, nev)
            lower_rows = pl.ds(width + spin * nev, nev)
            weights[upper_rows, :dil] = ap_re
            weights[upper_rows, dil:] = ap_im
            weights[lower_rows, :dil] = ap_im
            weights[lower_rows, dil:] = -ap_re

    def copy(src, slot, chunk, lane, target):
        at = pl.ds(pl.multiple_of(chunk * rows, rows), rows)
        return pltpu.make_async_remote_copy(
            src_ref=src.at[at],
            dst_ref=recv.at[slot, at],
            send_sem=send_sem.at[lane, chunk],
            recv_sem=recv_sem.at[slot, chunk],
            device_id=(target, mom),
            device_id_type=MESH,
        )

    def arrived(slot, chunk):
        copy(own, slot, chunk, 0, before).wait_recv()

    fill_weights(0)

    def make_own(chunk, carry):
        at = pl.ds(pl.multiple_of(chunk * rows, rows), rows)
        own[at, :] = dot(noise[at, :], weights[...]).astype(jnp.bfloat16)
        copy(own, 3, chunk, 0, before).start()

        @pl.when(upper == 1)
        def _():
            copy(own, 1, chunk, 1, across).start()

        @pl.when(odd == 1)
        def _():
            copy(own, 0, chunk, 2, sibling).start()

        return carry

    lax.fori_loop(0, chunks, make_own, 0)

    fill_weights(1)
    half = dil // 2

    def make_source(part, carry):
        at = pl.ds(pl.multiple_of(part * half, half), half)
        lower = pl.ds(pl.multiple_of(dil + part * half, half), half)
        meson = dot(noise[at, :], weights[...]).astype(jnp.bfloat16)
        re, im = meson[:, :dil], meson[:, dil:]
        source[at, :dil] = re
        source[at, dil:] = im
        source[lower, :dil] = -im
        source[lower, dil:] = re
        return carry

    lax.fori_loop(0, 2, make_source, 0)

    def finish(slot, chunk):
        at = pl.ds(pl.multiple_of(chunk * rows, rows), rows)
        block = dot(recv[slot, at, :], source[...]).astype(jnp.bfloat16)
        staged[slot, 0, at, :] = block[:, :dil]
        staged[slot, 1, at, :] = block[:, dil:]
        pltpu.make_async_copy(
            staged.at[slot, :, at], out_hbm.at[0, slot, 0, :, at], out_sem
        ).start()

    def step(chunk, carry):
        arrived(3, chunk)

        @pl.when(upper == 0)
        def _():
            copy(recv.at[3], 1, chunk, 1, across).start()

        @pl.when(odd == 0)
        def _():
            copy(recv.at[3], 2, chunk, 2, sibling).start()

        arrived(1, chunk)

        @pl.when(odd == 0)
        def _():
            copy(recv.at[1], 0, chunk, 3, sibling).start()

        @pl.when(odd == 1)
        def _():
            copy(recv.at[1], 2, chunk, 3, sibling).start()

        finish(3, chunk)
        finish(1, chunk)
        arrived(0, chunk)
        finish(0, chunk)
        arrived(2, chunk)
        finish(2, chunk)
        return carry

    lax.fori_loop(0, chunks, step, 0)

    for send in elem_sends:
        send.wait_send()

    def drain(chunk, carry):
        for lane in range(4):
            copy(own, 0, chunk, lane, before).wait_send()
        return carry

    lax.fori_loop(0, chunks, drain, 0)
    pltpu.make_async_copy(staged, out_hbm.at[0, :, 0], out_sem).wait()


def local(n_times, n_mom, sink_solutions, noise_sources, elementals, pairs):
    _, _, dil, width = sink_solutions.shape
    ops, _, _, nev, _ = elementals.shape
    chunks = CHUNKS
    bf16 = jnp.bfloat16
    flops = 2 * 2 * 4 * dil * width * (nev + dil) + NSEP * 2 * 4 * dil**3
    return pl.pallas_call(
        functools.partial(kernel, n_times, n_mom, chunks),
        out_shape=jax.ShapeDtypeStruct((1, NSEP, 1, 2, dil, dil), bf16),
        in_specs=[
            pl.BlockSpec(memory_space=pl.ANY),
            pl.BlockSpec(memory_space=pl.ANY),
            pl.BlockSpec(memory_space=pl.ANY),
            pl.BlockSpec(memory_space=pltpu.SMEM),
        ],
        out_specs=pl.BlockSpec(memory_space=pl.ANY),
        scratch_shapes=[
            pltpu.VMEM((2, dil, width), bf16),
            pltpu.VMEM((dil, 2 * width), bf16),
            pltpu.VMEM((n_mom * ops, 2, nev, nev), bf16),
            pltpu.VMEM((2 * width, 2 * dil), bf16),
            pltpu.VMEM((dil, 2 * dil), bf16),
            pltpu.VMEM((2 * dil, 2 * dil), bf16),
            pltpu.VMEM((NSEP, dil, 2 * dil), bf16),
            pltpu.VMEM((NSEP, 2, dil, dil), bf16),
            pltpu.SemaphoreType.DMA((4,)),
            pltpu.SemaphoreType.DMA((max(n_mom - 1, 1),)),
            pltpu.SemaphoreType.DMA((max(n_mom - 1, 1),)),
            pltpu.SemaphoreType.DMA((4, chunks)),
            pltpu.SemaphoreType.DMA((4, chunks)),
            pltpu.SemaphoreType.DMA,
        ],
        compiler_params=pltpu.CompilerParams(
            collective_id=0, has_side_effects=True, vmem_limit_bytes=40 * 1024 * 1024
        ),
        cost_estimate=pl.CostEstimate(
            flops=flops, bytes_accessed=2 * (4 * dil * width + 8 * dil * dil), transcendentals=0
        ),
    )(sink_solutions, noise_sources, elementals, pairs)


def solution(mesh):
    return jax.shard_map(
        functools.partial(local, mesh.shape["tm"], mesh.shape["mom"]),
        mesh=mesh,
        in_specs=(
            P("tm", None, None, None),
            P("tm", None, None, None),
            P("mom", "tm", None, None, None),
            P("mom", None),
        ),
        out_specs=P("tm", None, "mom", None, None, None),
        check_vma=False,
    )
```

time: 96.2 us -> 48.2 us (0.50)
  the two profiles are of different devices: /device:TPU:0 before, /device:TPU:5 now
where the time goes in v1:
time: 48.2 us; the launch traced here: 47.9 us
  Pallas kernels  42 us (87%)
  local copies, waits for them, and re-layouts  5.96 us (12%)
    pallas_call x1, Pallas kernels, local(): pl.pallas_call(functools.partial(kernel, n_times, n_mom, chunks), out_sha...  42 us
    unnamed x9, local copies, waits for them, and re-layouts  5.96 us

profile of v1, /device:TPU:5, one launch (start us, length us, event | category | flops | bytes accessed | tf_op | source)
XLA Modules:
  0.0 47.9 jit_solution(14114683379566995774)
XLA Ops:
  0.0 0.0 copy-start
  0.0 1.2 %copy-done = bf16[1,2,512,512]{3,2,1,0:T(8,128)(2,1)S(1)} copy-done((bf16[1,2,512,512]{3,2,1,0:T(8,128)(2,1)S(1)}, bf16[1,2,512,512]{3,2,1,0:T(8,128)(2,1)}, u32[]{:S(2)}) %copy-start) | copy-done | bytes 1048600
  1.2 0.0 copy-start.1
  1.2 1.2 %copy-done.1 = bf16[1,2,512,512]{3,2,1,0:T(8,128)(2,1)S(1)} copy-done((bf16[1,2,512,512]{3,2,1,0:T(8,128)(2,1)S(1)}, bf16[1,2,512,512]{3,2,1,0:T(8,128)(2,1)}, u32[]{:S(2)}) %copy-start.1) | copy-done | bytes 1048600
  2.5 0.0 copy-start.2
  2.5 0.8 %copy-done.2 = bf16[1,1,2,128,128]{4,3,2,1,0:T(8,128)(2,1)S(1)} copy-done((bf16[1,1,2,128,128]{4,3,2,1,0:T(8,128)(2,1)S(1)}, bf16[1,1,2,128,128]{4,3,2,1,0:T(8,128)(2,1)}, u32[]{:S(2)}) %copy-start.2) | copy-done | bytes 65560
  3.3 0.0 copy-start.3
  3.3 0.7 %copy-done.3 = s32[1,2]{1,0:T(1,128)S(1)} copy-done((s32[1,2]{1,0:T(1,128)S(1)}, s32[1,2]{1,0:T(1,128)}, u32[]{:S(2)}) %copy-start.3) | copy-done | bytes 32
  3.9 42.0 %shard_map.46 = bf16[1,4,1,2,512,512]{5,4,3,2,1,0:T(8,128)(2,1)S(1)} custom-call(bf16[1,2,512,512]{3,2,1,0:T(8,128)(2,1)S(1)} %copy-done, bf16[1,2,512,512]{3,2,1,0:T(8,128)(2,1)S(1)} %copy-done.1, bf16[1,1,2,128,128]{4,3,2,1,0:T(8,128)(2,1)S(1)} %copy-done.2, s32[1,2]{1,0:T(1,128)S(1)} %copy-done.3), custom_call_target="tpu_custom_call" | custom-call | flops 6979321856 | bytes 6291456 | tf_op jit(solution)/shard_map/pallas_call | solution.py:210
  45.9 2.0 %copy.6 = bf16[1,4,1,2,512,512]{5,4,3,2,1,0:T(8,128)(2,1)} copy(bf16[1,4,1,2,512,512]{5,4,3,2,1,0:T(8,128)(2,1)S(1)} %shard_map.46) | data formatting | bytes 8388608
Async XLA Ops:
  0.0 1.2 %copy-start = (bf16[1,2,512,512]{3,2,1,0:T(8,128)(2,1)S(1)}, bf16[1,2,512,512]{3,2,1,0:T(8,128)(2,1)}, u32[]{:S(2)}) copy-start(bf16[1,2,512,512]{3,2,1,0:T(8,128)(2,1)} %sink_hbm.1) | copy-start | bytes 3145732
  1.2 1.2 %copy-start.1 = (bf16[1,2,512,512]{3,2,1,0:T(8,128)(2,1)S(1)}, bf16[1,2,512,512]{3,2,1,0:T(8,128)(2,1)}, u32[]{:S(2)}) copy-start(bf16[1,2,512,512]{3,2,1,0:T(8,128)(2,1)} %noise_hbm.1) | copy-start | bytes 3145732
  2.5 0.8 %copy-start.2 = (bf16[1,1,2,128,128]{4,3,2,1,0:T(8,128)(2,1)S(1)}, bf16[1,1,2,128,128]{4,3,2,1,0:T(8,128)(2,1)}, u32[]{:S(2)}) copy-start(bf16[1,1,2,128,128]{4,3,2,1,0:T(8,128)(2,1)} %elem_hbm.1) | copy-start | bytes 196612
  3.3 0.7 %copy-start.3 = (s32[1,2]{1,0:T(1,128)S(1)}, s32[1,2]{1,0:T(1,128)}, u32[]{:S(2)}) copy-start(s32[1,2]{1,0:T(1,128)} %pairs_ref.1) | copy-start | bytes 28

commit v2 on v1

--- a/solution.py
+++ b/solution.py
@@ -9,7 +9,7 @@
 
 NSEP = 4
 MESH = pl.DeviceIdType.MESH
-CHUNKS = 8
+CHUNKS = 16
 
 
 def dot(left, right):
@@ -18,8 +18,8 @@
 
 def kernel(
     n_times, n_mom, chunks,
-    sink_hbm, noise_hbm, elem_hbm, pairs_ref, out_hbm,
-    sink, noise, elems, weights, own, source, recv, staged,
+    sink_hbm, noise_hbm, elem_hbm, pairs_hbm, out_hbm,
+    pairs_ref, sink, noise, elems, weights, own, source, recv, staged,
     load_sem, elem_send, elem_recv, send_sem, recv_sem, out_sem,
 ):
     time = lax.axis_index("tm")
@@ -42,6 +42,8 @@
         elem_hbm.at[:, 0], elems.at[pl.ds(mom * ops, ops)], load_sem.at[0]
     )
     own_elem.start()
+    pairs_load = pltpu.make_async_copy(pairs_hbm, pairs_ref, load_sem.at[4])
+    pairs_load.start()
     sink_load = pltpu.make_async_copy(sink_hbm.at[0], sink, load_sem.at[1])
     sink_load.start()
     noise_loads = [
@@ -74,6 +76,7 @@
         send.start()
         elem_sends.append(send)
     own_elem.wait()
+    pairs_load.wait()
     sink_load.wait()
     for send in elem_sends:
         send.wait_recv()
@@ -116,49 +119,39 @@
 
     fill_weights(0)
 
-    def make_own(chunk, carry):
-        at = pl.ds(pl.multiple_of(chunk * rows, rows), rows)
+    def send_own(chunk):
+        copy(own, 3, chunk, 0, before).start()
+
+        @pl.when(upper == 1)
+        def _():
+            copy(own, 1, chunk, 1, across).start()
+
+        @pl.when(odd == 1)
+        def _():
+            copy(own, 0, chunk, 2, sibling).start()
+
+    tall = 4 * rows
+
+    def make_own(part, carry):
+        at = pl.ds(pl.multiple_of(part * tall, tall), tall)
         own[at, :] = dot(noise[at, :], weights[...]).astype(jnp.bfloat16)
-        copy(own, 3, chunk, 0, before).start()
-
-        @pl.when(upper == 1)
-        def _():
-            copy(own, 1, chunk, 1, across).start()
-
-        @pl.when(odd == 1)
-        def _():
-            copy(own, 0, chunk, 2, sibling).start()
-
-        return carry
-
-    lax.fori_loop(0, chunks, make_own, 0)
-
-    fill_weights(1)
-    half = dil // 2
-
-    def make_source(part, carry):
-        at = pl.ds(pl.multiple_of(part * half, half), half)
-        lower = pl.ds(pl.multiple_of(dil + part * half, half), half)
+        for piece in range(4):
+            send_own(part * 4 + piece)
+        return carry
+
+    lax.fori_loop(0, dil // tall, make_own, 0)
+
+    def make_source(part):
+        at = pl.ds(pl.multiple_of(part * tall, tall), tall)
+        lower = pl.ds(pl.multiple_of(dil + part * tall, tall), tall)
         meson = dot(noise[at, :], weights[...]).astype(jnp.bfloat16)
         re, im = meson[:, :dil], meson[:, dil:]
         source[at, :dil] = re
         source[at, dil:] = im
         source[lower, :dil] = -im
         source[lower, dil:] = re
-        return carry
-
-    lax.fori_loop(0, 2, make_source, 0)
-
-    def finish(slot, chunk):
-        at = pl.ds(pl.multiple_of(chunk * rows, rows), rows)
-        block = dot(recv[slot, at, :], source[...]).astype(jnp.bfloat16)
-        staged[slot, 0, at, :] = block[:, :dil]
-        staged[slot, 1, at, :] = block[:, dil:]
-        pltpu.make_async_copy(
-            staged.at[slot, :, at], out_hbm.at[0, slot, 0, :, at], out_sem
-        ).start()
-
-    def step(chunk, carry):
+
+    def forward(chunk):
         arrived(3, chunk)
 
         @pl.when(upper == 0)
@@ -179,15 +172,45 @@
         def _():
             copy(recv.at[1], 2, chunk, 3, sibling).start()
 
-        finish(3, chunk)
-        finish(1, chunk)
-        arrived(0, chunk)
-        finish(0, chunk)
-        arrived(2, chunk)
-        finish(2, chunk)
-        return carry
-
-    lax.fori_loop(0, chunks, step, 0)
+    pair = 2 * rows
+
+    def finish(part):
+        at = pl.ds(pl.multiple_of(part * pair, pair), pair)
+        for piece in range(2):
+            arrived(0, part * 2 + piece)
+            arrived(2, part * 2 + piece)
+        later = recv[:, at, :].reshape(NSEP * pair, 2 * dil)
+        block = dot(later, source[...]).astype(jnp.bfloat16).reshape(NSEP, pair, 2 * dil)
+        staged[:, 0, at, :] = block[:, :, :dil]
+        staged[:, 1, at, :] = block[:, :, dil:]
+        pltpu.make_async_copy(staged.at[:, :, at], out_hbm.at[0, :, 0, :, at], out_sem).start()
+
+    forward(0)
+    fill_weights(1)
+
+    def with_source(part, carry):
+        forward(1 + part)
+        make_source(part)
+        return carry
+
+    lax.fori_loop(0, 4, with_source, 0)
+
+    def with_backlog(part, carry):
+        forward(5 + part)
+        finish(part)
+        return carry
+
+    lax.fori_loop(0, 4, with_backlog, 0)
+
+    def steady(part, carry):
+        forward(1 + 2 * part)
+        forward(2 + 2 * part)
+        finish(part)
+        return carry
+
+    lax.fori_loop(4, chunks // 2 - 1, steady, 0)
+    forward(chunks - 1)
+    finish(chunks // 2 - 1)
 
     for send in elem_sends:
         send.wait_send()
@@ -210,14 +233,10 @@
     return pl.pallas_call(
         functools.partial(kernel, n_times, n_mom, chunks),
         out_shape=jax.ShapeDtypeStruct((1, NSEP, 1, 2, dil, dil), bf16),
-        in_specs=[
-            pl.BlockSpec(memory_space=pl.ANY),
-            pl.BlockSpec(memory_space=pl.ANY),
-            pl.BlockSpec(memory_space=pl.ANY),
-            pl.BlockSpec(memory_space=pltpu.SMEM),
-        ],
+        in_specs=[pl.BlockSpec(memory_space=pltpu.HBM)] * 4,
         out_specs=pl.BlockSpec(memory_space=pl.ANY),
         scratch_shapes=[
+            pltpu.SMEM(pairs.shape, pairs.dtype),
             pltpu.VMEM((2, dil, width), bf16),
             pltpu.VMEM((dil, 2 * width), bf16),
             pltpu.VMEM((n_mom * ops, 2, nev, nev), bf16),
@@ -226,7 +245,7 @@
             pltpu.VMEM((2 * dil, 2 * dil), bf16),
             pltpu.VMEM((NSEP, dil, 2 * dil), bf16),
             pltpu.VMEM((NSEP, 2, dil, dil), bf16),
-            pltpu.SemaphoreType.DMA((4,)),
+            pltpu.SemaphoreType.DMA((5,)),
             pltpu.SemaphoreType.DMA((max(n_mom - 1, 1),)),
             pltpu.SemaphoreType.DMA((max(n_mom - 1, 1),)),
             pltpu.SemaphoreType.DMA((4, chunks)),
@@ -239,7 +258,12 @@
         cost_estimate=pl.CostEstimate(
             flops=flops, bytes_accessed=2 * (4 * dil * width + 8 * dil * dil), transcendentals=0
         ),
-    )(sink_solutions, noise_sources, elementals, pairs)
+    )(
+        *[
+            pltpu.with_memory_space_constraint(array, pltpu.HBM)
+            for array in (sink_solutions, noise_sources, elementals, pairs)
+        ]
+    )
 
 
 def solution(mesh):

time: 48.2 us -> 42 us (0.87)
  local copies, waits for them, and re-layouts: 5.96 us -> 2.02 us
  Pallas kernels: 42 us -> 39.8 us
    unnamed x9 -> x1, local copies, waits for them, and re-layouts: 5.96 us -> 2.02 us
    pallas_call x1, Pallas kernels: 42 us -> 39.8 us  [local(): pl.pallas_call(functools.partial(kernel, n_times, n_mom, chunks), out_sha...]
where the time goes in v2:
time: 42 us; the launch traced here: 41.8 us
  Pallas kernels  39.8 us (95%)
  local copies, waits for them, and re-layouts  2.02 us (5%)
    pallas_call x1, Pallas kernels, local(): pl.pallas_call(functools.partial(kernel, n_times, n_mom, chunks), out_sha...  39.8 us
    unnamed x1, local copies, waits for them, and re-layouts  2.02 us

profile of v2, /device:TPU:5, one launch (start us, length us, event | category | flops | bytes accessed | tf_op | source)
XLA Modules:
  0.0 41.8 jit_solution(8023150516936095364)
XLA Ops:
  0.0 39.8 %shard_map.46 = bf16[1,4,1,2,512,512]{5,4,3,2,1,0:T(8,128)(2,1)S(1)} custom-call(bf16[1,2,512,512]{3,2,1,0:T(8,128)(2,1)} %sink_hbm.1, bf16[1,2,512,512]{3,2,1,0:T(8,128)(2,1)} %noise_hbm.1, bf16[1,1,2,128,128]{4,3,2,1,0:T(8,128)(2,1)} %elem_hbm.1, s32[1,2]{1,0:T(1,128)} %pairs_hbm.1), custom_call_target="tpu_custom_call" | custom-call | flops 6979321856 | bytes 6291456 | tf_op jit(solution)/shard_map/pallas_call | solution.py:233
  39.8 2.0 %copy.6 = bf16[1,4,1,2,512,512]{5,4,3,2,1,0:T(8,128)(2,1)} copy(bf16[1,4,1,2,512,512]{5,4,3,2,1,0:T(8,128)(2,1)S(1)} %shard_map.46) | data formatting | bytes 8388608

commit v3 on v2

--- a/solution.py
+++ b/solution.py
@@ -10,6 +10,7 @@
 NSEP = 4
 MESH = pl.DeviceIdType.MESH
 CHUNKS = 16
+RELAYED = 2
 
 
 def dot(left, right):
@@ -19,8 +20,8 @@
 def kernel(
     n_times, n_mom, chunks,
     sink_hbm, noise_hbm, elem_hbm, pairs_hbm, out_hbm,
-    pairs_ref, sink, noise, elems, weights, own, source, recv, staged,
-    load_sem, elem_send, elem_recv, send_sem, recv_sem, out_sem,
+    pairs_ref, sink, noise, elems, weights, own, source, recv, staged, relay,
+    load_sem, elem_send, elem_recv, send_sem, recv_sem, relay_send, relay_recv, out_sem,
 ):
     time = lax.axis_index("tm")
     mom = lax.axis_index("mom")
@@ -130,16 +131,59 @@
         def _():
             copy(own, 0, chunk, 2, sibling).start()
 
-    tall = 4 * rows
-
-    def make_own(part, carry):
+    first_relayed = chunks - RELAYED
+
+    def to_relay(index):
+        return pltpu.make_async_remote_copy(
+            src_ref=own.at[pl.ds((first_relayed + index) * rows, rows)],
+            dst_ref=relay.at[pl.ds(index * rows, rows)],
+            send_sem=send_sem.at[1, first_relayed + index],
+            recv_sem=relay_recv.at[index],
+            device_id=(across, mom),
+            device_id_type=MESH,
+        )
+
+    def from_relay(index):
+        return pltpu.make_async_remote_copy(
+            src_ref=relay.at[pl.ds(index * rows, rows)],
+            dst_ref=recv.at[1, pl.ds((first_relayed + index) * rows, rows)],
+            send_sem=relay_send.at[index],
+            recv_sem=recv_sem.at[1, first_relayed + index],
+            device_id=(before, mom),
+            device_id_type=MESH,
+        )
+
+    per_part = 4
+    tall = per_part * rows
+    parts = dil // tall
+
+    def compute_own(part):
         at = pl.ds(pl.multiple_of(part * tall, tall), tall)
         own[at, :] = dot(noise[at, :], weights[...]).astype(jnp.bfloat16)
-        for piece in range(4):
-            send_own(part * 4 + piece)
-        return carry
-
-    lax.fori_loop(0, dil // tall, make_own, 0)
+
+    def make_own(part, carry):
+        compute_own(part)
+        for piece in range(per_part):
+            send_own(part * per_part + piece)
+        return carry
+
+    make_own(0, 0)
+    compute_own(parts - 1)
+
+    @pl.when(upper == 0)
+    def _():
+        for index in range(RELAYED):
+            to_relay(index).start()
+
+    lax.fori_loop(1, parts - 1, make_own, 0)
+    for piece in range(per_part):
+        send_own((parts - 1) * per_part + piece)
+
+    @pl.when(upper == 1)
+    def _():
+        for index in range(RELAYED):
+            to_relay(index).wait_recv()
+            from_relay(index).start()
 
     def make_source(part):
         at = pl.ds(pl.multiple_of(part * tall, tall), tall)
@@ -154,7 +198,7 @@
     def forward(chunk):
         arrived(3, chunk)
 
-        @pl.when(upper == 0)
+        @pl.when((upper == 0) & (chunk < first_relayed))
         def _():
             copy(recv.at[3], 1, chunk, 1, across).start()
 
@@ -209,8 +253,26 @@
         return carry
 
     lax.fori_loop(4, chunks // 2 - 1, steady, 0)
+    last = chunks // 2 - 1
+    at = pl.ds(last * pair, pair)
+
+    def finish_slots(slots):
+        later = jnp.concatenate([recv[slot, at, :] for slot in slots], axis=0)
+        block = dot(later, source[...]).astype(jnp.bfloat16)
+        for place, slot in enumerate(slots):
+            mine = block[place * pair : (place + 1) * pair]
+            staged[slot, 0, at, :] = mine[:, :dil]
+            staged[slot, 1, at, :] = mine[:, dil:]
+            pltpu.make_async_copy(
+                staged.at[slot, :, at], out_hbm.at[0, slot, 0, :, at], out_sem
+            ).start()
+
     forward(chunks - 1)
-    finish(chunks // 2 - 1)
+    finish_slots((1, 3))
+    for piece in range(2):
+        arrived(0, last * 2 + piece)
+        arrived(2, last * 2 + piece)
+    finish_slots((0, 2))
 
     for send in elem_sends:
         send.wait_send()
@@ -221,6 +283,12 @@
         return carry
 
     lax.fori_loop(0, chunks, drain, 0)
+
+    @pl.when(upper == 1)
+    def _():
+        for index in range(RELAYED):
+            from_relay(index).wait_send()
+
     pltpu.make_async_copy(staged, out_hbm.at[0, :, 0], out_sem).wait()
 
 
@@ -245,11 +313,14 @@
             pltpu.VMEM((2 * dil, 2 * dil), bf16),
             pltpu.VMEM((NSEP, dil, 2 * dil), bf16),
             pltpu.VMEM((NSEP, 2, dil, dil), bf16),
+            pltpu.VMEM((RELAYED * dil // chunks, 2 * dil), bf16),
             pltpu.SemaphoreType.DMA((5,)),
             pltpu.SemaphoreType.DMA((max(n_mom - 1, 1),)),
             pltpu.SemaphoreType.DMA((max(n_mom - 1, 1),)),
             pltpu.SemaphoreType.DMA((4, chunks)),
             pltpu.SemaphoreType.DMA((4, chunks)),
+            pltpu.SemaphoreType.DMA((RELAYED,)),
+            pltpu.SemaphoreType.DMA((RELAYED,)),
             pltpu.SemaphoreType.DMA,
         ],
         compiler_params=pltpu.CompilerParams(

time: 42 us -> 40.4 us (0.962)
  Pallas kernels: 39.8 us -> 38.2 us
    pallas_call x1, Pallas kernels: 39.8 us -> 38.2 us  [local(): pl.pallas_call(functools.partial(kernel, n_times, n_mom, chunks), out_sha...]
where the time goes in v3:
time: 40.4 us; the launch traced here: 40.3 us
  Pallas kernels  38.2 us (95%)
  local copies, waits for them, and re-layouts  2.02 us (5%)
    pallas_call x1, Pallas kernels, local(): pl.pallas_call(functools.partial(kernel, n_times, n_mom, chunks), out_sha...  38.2 us
    unnamed x1, local copies, waits for them, and re-layouts  2.02 us

profile of v3, /device:TPU:5, one launch (start us, length us, event | category | flops | bytes accessed | tf_op | source)
XLA Modules:
  0.0 40.3 jit_solution(9934200918217214534)
XLA Ops:
  0.0 38.2 %shard_map.46 = bf16[1,4,1,2,512,512]{5,4,3,2,1,0:T(8,128)(2,1)S(1)} custom-call(bf16[1,2,512,512]{3,2,1,0:T(8,128)(2,1)} %sink_hbm.1, bf16[1,2,512,512]{3,2,1,0:T(8,128)(2,1)} %noise_hbm.1, bf16[1,1,2,128,128]{4,3,2,1,0:T(8,128)(2,1)} %elem_hbm.1, s32[1,2]{1,0:T(1,128)} %pairs_hbm.1), custom_call_target="tpu_custom_call" | custom-call | flops 6979321856 | bytes 6291456 | tf_op jit(solution)/shard_map/pallas_call | solution.py:301
  38.3 2.0 %copy.6 = bf16[1,4,1,2,512,512]{5,4,3,2,1,0:T(8,128)(2,1)} copy(bf16[1,4,1,2,512,512]{5,4,3,2,1,0:T(8,128)(2,1)S(1)} %shard_map.46) | data formatting | bytes 8388608
